TPU v7x, 256 devices: a whole 4x4x8 slice. The times are simulated.
256 devices in a mesh: freq: 4 (over x), row: 8 (over y, core), col: 8 (over z).
Axes of the slice: x: 4, y: 4, z: 8, core: 2. Of those that a mesh axis runs over, the one named last changes fastest.
Arguments:
- operator: bfloat16 [4, 2, 12000, 12000], P('freq', None, 'row', 'col'), may hold values from -0.0390625 to 0.0390625
- recorded: bfloat16 [4, 2, 12000, 128], P('freq', None, 'row'), may hold values from -61 to 61
Outputs:
- solution: float32 [4, 2, 12000, 128], P('freq', None, 'col')
- residual: float32 [4, 2, 12000, 128], P('freq', None, 'row')
All inputs are finite; a program needn't handle non-finite values.
Results may differ from a plain program's by a relative error of at most 0.0044.
Values sent between devices are 32-bit elements; how exact they have to be, the bound alone decides.
A program may use at most 128 MiB of HBM per device.

v0:
```python
import jax
import jax.numpy as jnp
from jax import lax
from jax.sharding import PartitionSpec as P

ITERS = 2
epsilon = 1e-06


def forward_part(operator, vector):
    blocks = jnp.einsum("krc,lcs->klrs", operator[0], vector[0], preferred_element_type=jnp.float32)
    return jnp.stack([blocks[0, 0] - blocks[1, 1], blocks[0, 1] + blocks[1, 0]])[None]


def adjoint_part(operator, vector):
    blocks = jnp.einsum("krc,lrs->klcs", operator[0], vector[0], preferred_element_type=jnp.float32)
    return jnp.stack([blocks[0, 0] + blocks[1, 1], blocks[0, 1] - blocks[1, 0]])[None]


def forward_reduce(partial_value, left_vec, alpha_now):
    imaged = lax.psum(partial_value, "col")
    update = imaged - alpha_now * left_vec
    squares = lax.psum(jnp.sum(update * update), ("freq", "row"))
    return (imaged, update, jnp.sqrt(squares + epsilon))


def adjoint_reduce(partial_value, right_vec, beta_now):
    summed = lax.psum(partial_value, "row")
    update = summed - beta_now * right_vec
    squares = lax.psum(jnp.sum(update * update), ("freq", "col"))
    return (update, jnp.sqrt(squares + epsilon))


def shards(operator, recorded):
    observed = recorded.astype(jnp.float32)
    col_rows = operator.shape[3]
    sources = recorded.shape[3]
    beta_now = jnp.sqrt(lax.psum(jnp.sum(observed * observed), ("freq", "row")) + epsilon)
    left_vec = observed / beta_now
    right_vec = jnp.zeros((1, 2, col_rows, sources), jnp.float32)
    back, alpha_now = adjoint_reduce(
        adjoint_part(operator, left_vec.astype(jnp.bfloat16)), right_vec, beta_now
    )
    right_vec = back / alpha_now
    search = right_vec
    phi_bar = beta_now
    rho_bar = alpha_now
    solution = jnp.zeros((1, 2, col_rows, sources), jnp.float32)
    fitted = jnp.zeros_like(observed)
    search_image = fitted
    w_ratio = jnp.float32(0.0)
    for turn_index in range(ITERS):
        imaged, update, beta_now = forward_reduce(
            forward_part(operator, right_vec.astype(jnp.bfloat16)), left_vec, alpha_now
        )
        left_vec = update / beta_now
        if turn_index == 0:
            search_image = imaged
        else:
            search_image = imaged - w_ratio * search_image
        rho_now = jnp.sqrt(rho_bar * rho_bar + beta_now * beta_now)
        cosine = rho_bar / rho_now
        sine_val = beta_now / rho_now
        phi_now = cosine * phi_bar
        phi_bar = sine_val * phi_bar
        solution = solution + phi_now / rho_now * search
        fitted = fitted + phi_now / rho_now * search_image
        if turn_index + 1 < ITERS:
            back, alpha_now = adjoint_reduce(
                adjoint_part(operator, left_vec.astype(jnp.bfloat16)), right_vec, beta_now
            )
            right_vec = back / alpha_now
            w_ratio = sine_val * alpha_now / rho_now
            rho_bar = -cosine * alpha_now
            search = right_vec - w_ratio * search
    return (solution, observed - fitted)


def solution(mesh):
    in_specs = (P("freq", None, "row", "col"), P("freq", None, "row", None))
    out_specs = (P("freq", None, "col", None), P("freq", None, "row", None))
    return jax.shard_map(shards, mesh=mesh, in_specs=in_specs, out_specs=out_specs, check_vma=False)
```

profile of v0, /device:TPU:1, one launch (start us, length us, event | category | flops | bytes accessed | tf_op | source)
XLA Modules:
  0.0 721.2 jit_solution(233663717337705087)
XLA Ops:
  7.2 0.0 all-reduce.5.cloned.1.call-start
  7.2 2.1 fusion.20
  9.3 65.9 %psum.63 = f32[]{:T(128)} all-reduce(f32[]{:T(128)} %fusion.20), channel_id=1, replica_groups=mesh['freq'=4,'row'=8,'col'=8] {'freq','row'}, use_global_device_ids=true, to_apply=%region_1.0 | all-reduce | flops 1 | bytes 8 | tf_op jit(solution)/shard_map/psum | solution.py:38
  75.9 0.0 copy-start.2
  75.9 23.8 %copy.5 = bf16[2,1500,1500]{1,2,0:T(8,128)(2,1)} copy(bf16[2,1500,1500]{2,0,1:T(2,128)(2,1)} %bitcast.70) | data formatting | bytes 18000000 | tf_op jit(solution)/shard_map/squeeze | solution.py:16
  99.7 0.0 copy-done.2
  99.7 6.3 fusion.17
  106.0 0.1 fusion.30
  106.1 0.1 fusion.32
  106.2 1.2 maximum_bitcast_fusion
  107.5 0.0 all-reduce.5.cloned.1.call-update
  107.5 0.0 all-reduce.7.cloned.1.call-start
  107.5 67.9 %all-reduce.5.cloned.1.call-done = f32[1,2,1500,128]{3,2,1,0:T(8,128)} async-done(((f32[1,2,1500,128]{3,2,1,0:T(8,128)}), f32[1,2,1500,128]{3,2,1,0:T(8,128)}) %all-reduce.5.cloned.1.call-update) | async-done | bytes 1536016 | tf_op jit(solution)/shard_map/psum | solution.py:28
  175.4 0.0 copy-start
  175.4 2.5 multiply_reduce_fusion.3
  177.9 61.5 %psum.65 = f32[]{:T(128)} all-reduce(f32[]{:T(128)} %multiply_reduce_fusion.3), channel_id=1, replica_groups=mesh['freq'=4,'row'=8,'col'=8] {'freq','col'}, use_global_device_ids=true, to_apply=%region_4.0 | all-reduce | flops 1 | bytes 8 | tf_op jit(solution)/shard_map/psum | solution.py:30
  240.1 0.0 copy-done
  240.1 6.3 fusion.8
  246.5 0.2 fusion.29
  246.6 1.2 maximum_bitcast_fusion.1
  247.9 0.0 all-reduce.7.cloned.1.call-update
  247.9 0.0 all-reduce.9.cloned.1.call-start
  247.9 82.4 %all-reduce.7.cloned.1.call-done = f32[1,2,1500,128]{3,2,1,0:T(8,128)} async-done(((f32[1,2,1500,128]{3,2,1,0:T(8,128)}), f32[1,2,1500,128]{3,2,1,0:T(8,128)}) %all-reduce.7.cloned.1.call-update) | async-done | bytes 1536016 | tf_op jit(solution)/shard_map/psum | solution.py:21
  330.4 0.0 copy-start.1
  330.4 2.7 multiply_reduce_fusion.2
  333.1 67.5 %psum.67 = f32[]{:T(128)} all-reduce(f32[]{:T(128)} %multiply_reduce_fusion.2), channel_id=1, replica_groups=mesh['freq'=4,'row'=8,'col'=8] {'freq','row'}, use_global_device_ids=true, to_apply=%region_7.0 | all-reduce | flops 1 | bytes 8 | tf_op jit(solution)/shard_map/psum | solution.py:23
  401.3 0.0 copy-done.1
  401.3 8.2 %fusion.14 = f32[2,2,1500,128]{3,2,1,0:T(8,128)S(1)} fusion(bf16[2,1500,1500,1]{2,0,1,3:T(2,128)(2,1)} %bitcast.72, f32[]{:T(128)S(6)} %sqrt.23, f32[1,2,1500,128]{3,2,1,0:T(8,128)S(1)} %copy-done.1, f32[]{:T(128)S(6)} %sqrt.22, f32[]{:T(128)S(6)} %sqrt.21, bf16[1,2,1500,128]{3,1,2,0:T(2,128)(2,1)} %param.3), kind=kOutput, calls=%fused_computation.10 | convolution fusion | flops 2306304000 | bytes 14376012 | tf_op jit(solution)/shard_map/krc,lrs->klcs/dot_general | solution.py:16
  409.5 0.2 fusion.27
  409.6 1.2 maximum_bitcast_fusion.2
  410.9 0.0 all-reduce.9.cloned.1.call-update
  410.9 0.0 all-reduce.11.cloned.1.call-start
  411.0 61.3 %all-reduce.9.cloned.1.call-done = f32[1,2,1500,128]{3,2,1,0:T(8,128)} async-done(((f32[1,2,1500,128]{3,2,1,0:T(8,128)}), f32[1,2,1500,128]{3,2,1,0:T(8,128)}) %all-reduce.9.cloned.1.call-update) | async-done | bytes 1536016 | tf_op jit(solution)/shard_map/psum | solution.py:28
  472.2 2.4 multiply_reduce_fusion.1
  474.6 61.5 %psum.69 = f32[]{:T(128)} all-reduce(f32[]{:T(128)} %multiply_reduce_fusion.1), channel_id=1, replica_groups=mesh['freq'=4,'row'=8,'col'=8] {'freq','col'}, use_global_device_ids=true, to_apply=%region_10.0 | all-reduce | flops 1 | bytes 8 | tf_op jit(solution)/shard_map/psum | solution.py:30
  536.8 6.9 fusion.11
  543.7 0.2 fusion.25
  543.9 1.2 maximum_bitcast_fusion.3
  545.1 0.0 all-reduce.11.cloned.1.call-update
  545.3 82.4 %all-reduce.11.cloned.1.call-done = f32[1,2,1500,128]{3,2,1,0:T(8,128)} async-done(((f32[1,2,1500,128]{3,2,1,0:T(8,128)}), f32[1,2,1500,128]{3,2,1,0:T(8,128)}) %all-reduce.11.cloned.1.call-update) | async-done | bytes 1536016 | tf_op jit(solution)/shard_map/psum | solution.py:21
  627.7 2.6 multiply_reduce_fusion
  630.4 67.6 %psum.71 = f32[]{:T(128)} all-reduce(f32[]{:T(128)} %multiply_reduce_fusion), channel_id=1, replica_groups=mesh['freq'=4,'row'=8,'col'=8] {'freq','row'}, use_global_device_ids=true, to_apply=%region_13.0 | all-reduce | flops 1 | bytes 8 | tf_op jit(solution)/shard_map/psum | solution.py:23
  698.8 3.0 convert_subtract_fusion
  701.8 6.4 copy.14
  708.2 6.4 copy.15
Async XLA Ops:
  7.2 168.3 %all-reduce.5.cloned.1.call-start = ((), (), s32[]{:S(2)}) async-start(), calls=%async_computation | async-start | bytes 3080192 | tf_op jit(solution)/shard_map/psum | solution.py:28
  75.9 23.8 %copy-start.2 = (bf16[1,2,1500,128]{3,1,2,0:T(2,128)(2,1)S(1)}, bf16[1,2,1500,128]{3,1,2,0:T(2,128)(2,1)}, u32[]{:S(2)}) copy-start(bf16[1,2,1500,128]{3,1,2,0:T(2,128)(2,1)} %param.3) | copy-start | bytes 2304004
  107.5 222.9 %all-reduce.7.cloned.1.call-start = ((), (), s32[]{:S(2)}) async-start(), calls=%async_computation.1 | async-start | bytes 3080192 | tf_op jit(solution)/shard_map/psum | solution.py:21
  175.4 64.7 %copy-start = (f32[1,2,1500,128]{3,2,1,0:T(8,128)S(1)}, f32[1,2,1500,128]{3,2,1,0:T(8,128)}, u32[]{:S(2)}) copy-start(f32[1,2,1500,128]{3,2,1,0:T(8,128)} %all-reduce.5.cloned.1.call-done) | copy-start | bytes 4608004
  247.9 224.4 %all-reduce.9.cloned.1.call-start = ((), (), s32[]{:S(2)}) async-start(), calls=%async_computation.2 | async-start | bytes 3080192 | tf_op jit(solution)/shard_map/psum | solution.py:28
  330.4 70.9 %copy-start.1 = (f32[1,2,1500,128]{3,2,1,0:T(8,128)S(1)}, f32[1,2,1500,128]{3,2,1,0:T(8,128)}, u32[]{:S(2)}) copy-start(f32[1,2,1500,128]{3,2,1,0:T(8,128)} %all-reduce.7.cloned.1.call-done) | copy-start | bytes 4608004
  410.9 216.8 %all-reduce.11.cloned.1.call-start = ((), (), s32[]{:S(2)}) async-start(), calls=%async_computation.3 | async-start | bytes 3080192 | tf_op jit(solution)/shard_map/psum | solution.py:21
Sparse Core Ops, SparseCore 0:
  107.6 67.7 all-reduce.4
  248.0 82.3 all-reduce.6
  411.0 61.1 all-reduce.8
  545.3 82.3 all-reduce.10
where the time goes:
time: 722 us; the launch traced here: 721 us
  blocking collectives  324 us (45%)
  waiting for transfers between devices  294 us (41%)
  local copies, waits for them, and re-layouts  36.7 us (5%)
  matrix products  27.7 us (4%)
  other arithmetic  20.9 us (3%)
  between operations  17.7 us (2%)
    psum x2, waiting for transfers between devices, forward_reduce(): imaged = lax.psum(partial_value, 'col')  165 us
    psum x2, blocking collectives, forward_reduce(): squares = lax.psum(jnp.sum(update * update), ('freq', 'row'))  135 us
    psum x2, waiting for transfers between devices, adjoint_reduce(): summed = lax.psum(partial_value, 'row')  129 us
    psum x2, blocking collectives, adjoint_reduce(): squares = lax.psum(jnp.sum(update * update), ('freq', 'col'))  123 us
    psum x1, blocking collectives, shards(): lax.psum(jnp.sum(observed * observed), ('freq', 'row')) + epsilon  65.9 us
    squeeze x1, local copies, waits for them, and re-layouts, adjoint_part(): operator[0]  23.8 us
    dot_general x2, matrix products, adjoint_part(): jnp.einsum('krc,lrs->klcs', operator[0], vector[0], preferred_element_typ...  14.5 us
  transfers between devices with their start and end apart: 4, of which 4 were waited for; matrix products, arithmetic and copies ran while one was open for 0% of the time, Pallas kernels for 0%

commit v1 on v0

--- a/solution.py
+++ b/solution.py
@@ -18,7 +18,9 @@
 
 
 def forward_reduce(partial_value, left_vec, alpha_now):
-    imaged = lax.psum(partial_value, "col")
+    imaged = partial_value
+    for hop in (1, 2, 4):
+        imaged = imaged + lax.ppermute(imaged, "col", [(dev, dev ^ hop) for dev in range(8)])
     update = imaged - alpha_now * left_vec
     squares = lax.psum(jnp.sum(update * update), ("freq", "row"))
     return (imaged, update, jnp.sqrt(squares + epsilon))

time: 722 us -> 976 us (1.35)
  blocking collectives: 324 us -> 467 us
  waiting for transfers between devices: 294 us -> 362 us
  local copies, waits for them, and re-layouts: 36.7 us -> 71 us
    ppermute x0 -> x6, waiting for transfers between devices: none -> 233 us  [forward_reduce(): lax.ppermute(imaged, 'col', [(dev, dev ^ hop) for dev in range(8)])]
    psum x2 -> x0, waiting for transfers between devices: 165 us -> none  [forward_reduce(): imaged = lax.psum(partial_value, 'col')]
    psum x2, blocking collectives: 135 us -> 278 us  [forward_reduce(): squares = lax.psum(jnp.sum(update * update), ('freq', 'row'))]
    add x0 -> x4, local copies, waits for them, and re-layouts: none -> 23.2 us  [forward_reduce(): imaged + lax.ppermute(imaged, 'col', [(dev, dev ^ hop) for dev in range(8)])]
    broadcast_in_dim x0 -> x2, local copies, waits for them, and re-layouts: none -> 11.2 us  [forward_part(): jnp.stack([blocks[0, 0] - blocks[1, 1], blocks[0, 1] + blocks[1, 0]])[None]]
  transfers between devices with their start and end apart: 4 -> 8, of which waited for: 4 -> 8; matrix products, arithmetic and copies ran while one was open for 0% -> 0% of each run, Pallas kernels for 0% -> 0%
where the time goes in v1:
time: 976 us; the launch traced here: 968 us
  blocking collectives  467 us (48%)
  waiting for transfers between devices  362 us (37%)
  local copies, waits for them, and re-layouts  71 us (7%)
  matrix products  27.8 us (3%)
  other arithmetic  20.4 us (2%)
  between operations  18.5 us (2%)
    psum x2, blocking collectives, forward_reduce(): squares = lax.psum(jnp.sum(update * update), ('freq', 'row'))  278 us
    ppermute x6, waiting for transfers between devices, forward_reduce(): lax.ppermute(imaged, 'col', [(dev, dev ^ hop) for dev in range(8)])  233 us
    psum x2, waiting for transfers between devices, adjoint_reduce(): summed = lax.psum(partial_value, 'row')  129 us
    psum x2, blocking collectives, adjoint_reduce(): squares = lax.psum(jnp.sum(update * update), ('freq', 'col'))  123 us
    psum x1, blocking collectives, shards(): lax.psum(jnp.sum(observed * observed), ('freq', 'row')) + epsilon  65.9 us
    squeeze x1, local copies, waits for them, and re-layouts, adjoint_part(): operator[0]  23.8 us
    add x4, local copies, waits for them, and re-layouts, forward_reduce(): imaged + lax.ppermute(imaged, 'col', [(dev, dev ^ hop) for dev in range(8)])  23.2 us
  transfers between devices with their start and end apart: 8, of which 8 were waited for; matrix products, arithmetic and copies ran while one was open for 0% of the time, Pallas kernels for 0%

profile of v1, /device:TPU:1, one launch (start us, length us, event | category | flops | bytes accessed | tf_op | source)
XLA Modules:
  0.0 967.6 jit_solution(16520764156395710637)
XLA Ops:
  7.2 2.1 fusion.20
  9.3 65.9 %psum.49 = f32[]{:T(128)} all-reduce(f32[]{:T(128)} %fusion.20), channel_id=1, replica_groups=mesh['freq'=4,'row'=8,'col'=8] {'freq','row'}, use_global_device_ids=true, to_apply=%region_1.0 | all-reduce | flops 1 | bytes 8 | tf_op jit(solution)/shard_map/psum | solution.py:40
  75.9 23.8 %copy.17 = bf16[2,1500,1500]{1,2,0:T(8,128)(2,1)} copy(bf16[2,1500,1500]{2,0,1:T(2,128)(2,1)} %bitcast.78) | data formatting | bytes 18000000 | tf_op jit(solution)/shard_map/squeeze | solution.py:16
  99.7 6.3 fusion.17
  106.2 1.2 maximum_bitcast_fusion
  107.5 67.9 %all-reduce.3.cloned.1.call-done = f32[1,2,1500,128]{3,2,1,0:T(8,128)} async-done(((f32[1,2,1500,128]{3,2,1,0:T(8,128)}), f32[1,2,1500,128]{3,2,1,0:T(8,128)}) %all-reduce.3.cloned.1.call-update) | async-done | bytes 1536016 | tf_op jit(solution)/shard_map/psum | solution.py:30
  175.4 2.5 multiply_reduce_fusion.3
  177.9 61.5 %psum.51 = f32[]{:T(128)} all-reduce(f32[]{:T(128)} %multiply_reduce_fusion.3), channel_id=1, replica_groups=mesh['freq'=4,'row'=8,'col'=8] {'freq','col'}, use_global_device_ids=true, to_apply=%region_4.0 | all-reduce | flops 1 | bytes 8 | tf_op jit(solution)/shard_map/psum | solution.py:32
  240.1 6.3 fusion.8
  246.5 0.2 fusion.29
  246.6 0.1 maximum_bitcast_fusion.1
  246.7 5.6 copy.22
  252.3 0.6 collective-permute-start
  252.9 18.9 %collective-permute-done = f32[1,2,1500,128]{3,1,2,0:T(2,128)S(1)} collective-permute-done((f32[1,2,1500,128]{3,1,2,0:T(2,128)S(1)}, f32[1,2,1500,128]{3,1,2,0:T(2,128)S(1)}, u32[]{:S(2)}, u32[]{:S(2)}) %collective-permute-start) | collective-permute-done | bytes 1536032 | tf_op jit(solution)/shard_map/ppermute | solution.py:23
  271.8 0.2 copy_add_fusion.5
  272.0 5.6 copy.24
  277.6 0.1 collective-permute-start.1
  277.7 60.5 %collective-permute-done.1 = f32[1,2,1500,128]{3,1,2,0:T(2,128)S(1)} collective-permute-done((f32[1,2,1500,128]{3,1,2,0:T(2,128)S(1)}, f32[1,2,1500,128]{3,1,2,0:T(2,128)S(1)}, u32[]{:S(2)}, u32[]{:S(2)}) %collective-permute-start.1) | collective-permute-done | bytes 1536032 | tf_op jit(solution)/shard_map/ppermute | solution.py:23
  338.1 0.3 copy_add_fusion.4
  338.4 5.6 copy.26
  344.0 0.1 collective-permute-start.2
  344.1 37.7 %collective-permute-done.2 = f32[1,2,1500,128]{3,1,2,0:T(2,128)S(1)} collective-permute-done((f32[1,2,1500,128]{3,1,2,0:T(2,128)S(1)}, f32[1,2,1500,128]{3,1,2,0:T(2,128)S(1)}, u32[]{:S(2)}, u32[]{:S(2)}) %collective-permute-start.2) | collective-permute-done | bytes 1536032 | tf_op jit(solution)/shard_map/ppermute | solution.py:23
  381.9 2.2 multiply_reduce_fusion.2
  384.1 138.3 %psum.52 = f32[]{:T(128)} all-reduce(f32[]{:T(128)} %get-tuple-element.6), channel_id=1, replica_groups=mesh['freq'=4,'row'=8,'col'=8] {'freq','row'}, use_global_device_ids=true, to_apply=%region_6.0 | all-reduce | flops 1 | bytes 8 | tf_op jit(solution)/shard_map/psum | solution.py:25
  523.1 8.3 fusion.14
  531.4 0.2 fusion.27
  531.6 1.3 maximum_bitcast_fusion.2
  532.9 60.7 %all-reduce.5.cloned.1.call-done = f32[1,2,1500,128]{3,2,1,0:T(8,128)} async-done(((f32[1,2,1500,128]{3,2,1,0:T(8,128)}), f32[1,2,1500,128]{3,2,1,0:T(8,128)}) %all-reduce.5.cloned.1.call-update) | async-done | bytes 1536016 | tf_op jit(solution)/shard_map/psum | solution.py:30
  593.5 2.4 multiply_reduce_fusion.1
  595.9 61.5 %psum.54 = f32[]{:T(128)} all-reduce(f32[]{:T(128)} %multiply_reduce_fusion.1), channel_id=1, replica_groups=mesh['freq'=4,'row'=8,'col'=8] {'freq','col'}, use_global_device_ids=true, to_apply=%region_9.0 | all-reduce | flops 1 | bytes 8 | tf_op jit(solution)/shard_map/psum | solution.py:32
  658.1 6.9 fusion.11
  665.0 0.2 fusion.25
  665.2 0.1 maximum_bitcast_fusion.3
  665.3 5.6 copy.32
  670.9 0.3 collective-permute-start.3
  671.2 18.9 %collective-permute-done.3 = f32[1,2,1500,128]{3,1,2,0:T(2,128)S(1)} collective-permute-done((f32[1,2,1500,128]{3,1,2,0:T(2,128)S(1)}, f32[1,2,1500,128]{3,1,2,0:T(2,128)S(1)}, u32[]{:S(2)}, u32[]{:S(2)}) %collective-permute-start.3) | collective-permute-done | bytes 1536032 | tf_op jit(solution)/shard_map/ppermute | solution.py:23
  690.0 0.2 copy_add_fusion.2
  690.2 5.6 copy.34
  695.8 0.1 collective-permute-start.4
  695.9 60.5 %collective-permute-done.4 = f32[1,2,1500,128]{3,1,2,0:T(2,128)S(1)} collective-permute-done((f32[1,2,1500,128]{3,1,2,0:T(2,128)S(1)}, f32[1,2,1500,128]{3,1,2,0:T(2,128)S(1)}, u32[]{:S(2)}, u32[]{:S(2)}) %collective-permute-start.4) | collective-permute-done | bytes 1536032 | tf_op jit(solution)/shard_map/ppermute | solution.py:23
  756.4 0.3 copy_add_fusion.1
  756.7 6.4 copy.36
  763.3 36.9 %collective-permute-done.5 = f32[1,2,1500,128]{3,1,2,0:T(2,128)} collective-permute-done((f32[1,2,1500,128]{3,1,2,0:T(2,128)}, f32[1,2,1500,128]{3,1,2,0:T(2,128)}, u32[]{:S(2)}, u32[]{:S(2)}) %collective-permute-start.5) | collective-permute-done | bytes 1536032 | tf_op jit(solution)/shard_map/ppermute | solution.py:23
  800.2 2.9 multiply_reduce_fusion
  803.1 139.6 %psum.55 = f32[]{:T(128)} all-reduce(f32[]{:T(128)} %multiply_reduce_fusion), channel_id=1, replica_groups=mesh['freq'=4,'row'=8,'col'=8] {'freq','row'}, use_global_device_ids=true, to_apply=%region_11.0 | all-reduce | flops 1 | bytes 8 | tf_op jit(solution)/shard_map/psum | solution.py:25
  943.5 4.0 convert_subtract_fusion
  947.5 6.4 copy.38
  953.9 6.4 copy.39
  (15 shorter events, 0.3 us)
Async XLA Ops:
  7.2 168.2 %all-reduce.3.cloned.1.call-start = ((), (), s32[]{:S(2)}) async-start(), calls=%async_computation | async-start | bytes 3080192 | tf_op jit(solution)/shard_map/psum | solution.py:30
  75.9 23.8 %copy-start.1 = (bf16[1,2,1500,128]{3,1,2,0:T(2,128)(2,1)S(1)}, bf16[1,2,1500,128]{3,1,2,0:T(2,128)(2,1)}, u32[]{:S(2)}) copy-start(bf16[1,2,1500,128]{3,1,2,0:T(2,128)(2,1)} %param.3) | copy-start | bytes 2304004
  107.5 486.1 %all-reduce.5.cloned.1.call-start = ((), (), s32[]{:S(2)}) async-start(), calls=%async_computation.1 | async-start | bytes 3080192 | tf_op jit(solution)/shard_map/psum | solution.py:30
  175.4 64.7 %copy-start = (f32[1,2,1500,128]{3,2,1,0:T(8,128)S(1)}, f32[1,2,1500,128]{3,2,1,0:T(8,128)}, u32[]{:S(2)}) copy-start(f32[1,2,1500,128]{3,2,1,0:T(8,128)} %all-reduce.3.cloned.1.call-done) | copy-start | bytes 4608004
  252.3 19.5 %collective-permute-start = (f32[1,2,1500,128]{3,1,2,0:T(2,128)S(1)}, f32[1,2,1500,128]{3,1,2,0:T(2,128)S(1)}, u32[]{:S(2)}, u32[]{:S(2)}) collective-permute-start(f32[1,2,1500,128]{3,1,2,0:T(2,128)S(1)} %copy.22), channel_id=1, source_target_pairs={{0,1},{1,0},{2,3},{3,2},{4,5},{5,4},{6,7},{7,6},{8,9},{9,8},{10,11... | collective-permute-start | bytes 4608008 | tf_op jit(solution)/shard_map/ppermute | solution.py:23
  277.6 60.6 %collective-permute-start.1 = (f32[1,2,1500,128]{3,1,2,0:T(2,128)S(1)}, f32[1,2,1500,128]{3,1,2,0:T(2,128)S(1)}, u32[]{:S(2)}, u32[]{:S(2)}) collective-permute-start(f32[1,2,1500,128]{3,1,2,0:T(2,128)S(1)} %copy.24), channel_id=1, source_target_pairs={{0,2},{1,3},{2,0},{3,1},{4,6},{5,7},{6,4},{7,5},{8,10},{9,11},{10,... | collective-permute-start | bytes 4608008 | tf_op jit(solution)/shard_map/ppermute | solution.py:23
  338.4 43.4 %copy-start.2 = (bf16[1,2,1500,128]{3,1,2,0:T(2,128)(2,1)S(1)}, bf16[1,2,1500,128]{3,1,2,0:T(2,128)(2,1)}, u32[]{:S(2)}) copy-start(bf16[1,2,1500,128]{3,1,2,0:T(2,128)(2,1)} %param.3) | copy-start | bytes 2304004
  344.0 37.8 %collective-permute-start.2 = (f32[1,2,1500,128]{3,1,2,0:T(2,128)S(1)}, f32[1,2,1500,128]{3,1,2,0:T(2,128)S(1)}, u32[]{:S(2)}, u32[]{:S(2)}) collective-permute-start(f32[1,2,1500,128]{3,1,2,0:T(2,128)S(1)} %copy.26), channel_id=1, source_target_pairs={{0,4},{1,5},{2,6},{3,7},{4,0},{5,1},{6,2},{7,3},{8,12},{9,13},{10,... | collective-permute-start | bytes 4608008 | tf_op jit(solution)/shard_map/ppermute | solution.py:23
  381.9 2.2 copy-start.3
  670.9 19.2 %collective-permute-start.3 = (f32[1,2,1500,128]{3,1,2,0:T(2,128)S(1)}, f32[1,2,1500,128]{3,1,2,0:T(2,128)S(1)}, u32[]{:S(2)}, u32[]{:S(2)}) collective-permute-start(f32[1,2,1500,128]{3,1,2,0:T(2,128)S(1)} %copy.32), channel_id=1, source_target_pairs={{0,1},{1,0},{2,3},{3,2},{4,5},{5,4},{6,7},{7,6},{8,9},{9,8},{10,11... | collective-permute-start | bytes 4608008 | tf_op jit(solution)/shard_map/ppermute | solution.py:23
  695.8 60.6 %collective-permute-start.4 = (f32[1,2,1500,128]{3,1,2,0:T(2,128)S(1)}, f32[1,2,1500,128]{3,1,2,0:T(2,128)S(1)}, u32[]{:S(2)}, u32[]{:S(2)}) collective-permute-start(f32[1,2,1500,128]{3,1,2,0:T(2,128)S(1)} %copy.34), channel_id=1, source_target_pairs={{0,2},{1,3},{2,0},{3,1},{4,6},{5,7},{6,4},{7,5},{8,10},{9,11},{10,... | collective-permute-start | bytes 4608008 | tf_op jit(solution)/shard_map/ppermute | solution.py:23
  763.1 37.1 %collective-permute-start.5 = (f32[1,2,1500,128]{3,1,2,0:T(2,128)}, f32[1,2,1500,128]{3,1,2,0:T(2,128)}, u32[]{:S(2)}, u32[]{:S(2)}) collective-permute-start(f32[1,2,1500,128]{3,1,2,0:T(2,128)} %copy.36), channel_id=1, source_target_pairs={{0,4},{1,5},{2,6},{3,7},{4,0},{5,1},{6,2},{7,3},{8,12},{9,13},{10,... | collective-permute-start | bytes 4608008 | tf_op jit(solution)/shard_map/ppermute | solution.py:23
Sparse Core Ops, SparseCore 0:
  107.6 67.7 all-reduce.2
  533.0 60.5 all-reduce.4
